TPU v7x, 128 devices: a whole 4x4x4 slice. The times are simulated.
128 devices in a mesh: dom: 8 (over z, core), slab: 16 (over x, y).
Axes of the slice: x: 4, y: 4, z: 4, core: 2. Of those that a mesh axis runs over, the one named last changes fastest.
Arguments:
- nodes: bfloat16 [8, 16, 512, 128], P('dom', 'slab'), may hold values from -6 to 6
- edges: bfloat16 [8, 16, 8192, 128], P('dom', 'slab'), may hold values from -6 to 6
- coarse: bfloat16 [8, 16, 128, 128], P('dom', 'slab'), may hold values from -6 to 6
- senders: int32 [8, 16, 8192], P('dom', 'slab'), may hold values from 0 to 767
- receivers: int32 [8, 16, 8192], P('dom', 'slab'), may hold values from 0 to 511
- mirror_rows: int32 [8, 16, 4, 64], P('dom', 'slab'), may hold values from 0 to 511
- owner_device: int32 [8, 16, 512, 1], P('dom', 'slab'), may hold values from 0 to 127; in each aligned block of 512 rows (0 to 511, 512 to 1023, ..., all dimensions but the last counted through in order) at most 8 rows name the same one
- owner_slot: int32 [8, 16, 512], P('dom', 'slab'), may hold values from 0 to 127
- edge_first: bfloat16 [384, 128], replicated, may hold values from -0.3125 to 0.3125
- edge_bias: float32 [128], replicated, may hold values from -3 to 3
- edge_second: bfloat16 [128, 128], replicated, may hold values from -0.5 to 0.5
- edge_gain: float32 [128], replicated, may hold values from 0.1 to 1.9
- node_first: bfloat16 [256, 128], replicated, may hold values from -0.375 to 0.375
- node_bias: float32 [128], replicated, may hold values from -3 to 3
- node_second: bfloat16 [128, 128], replicated, may hold values from -0.5 to 0.5
- node_gain: float32 [128], replicated, may hold values from 0.1 to 1.9
- coarse_first: bfloat16 [256, 128], replicated, may hold values from -0.375 to 0.375
- coarse_bias: float32 [128], replicated, may hold values from -3 to 3
- coarse_second: bfloat16 [128, 128], replicated, may hold values from -0.5 to 0.5
- coarse_gain: float32 [128], replicated, may hold values from 0.1 to 1.9
- cot_nodes: bfloat16 [8, 16, 512, 128], P('dom', 'slab'), may hold values from -6 to 6
- cot_edges: bfloat16 [8, 16, 8192, 128], P('dom', 'slab'), may hold values from -6 to 6
- cot_coarse: bfloat16 [8, 16, 128, 128], P('dom', 'slab'), may hold values from -18 to 18
Outputs:
- new_nodes: bfloat16 [8, 16, 512, 128], P('dom', 'slab')
- new_edges: bfloat16 [8, 16, 8192, 128], P('dom', 'slab')
- new_coarse: bfloat16 [8, 16, 128, 128], P('dom', 'slab')
- grad_nodes: float32 [8, 16, 512, 128], P('dom', 'slab')
- grad_edges: float32 [8, 16, 8192, 128], P('dom', 'slab')
- grad_coarse: float32 [8, 16, 128, 128], P('dom', 'slab')
Inputs may be any that keep to these rules, and one draw needn't show every extreme that they name: `owner_device`: among the rows of one partition no owner group is named more than 8 times, and some partition names one group exactly 8 times.
All inputs are finite; a program needn't handle non-finite values.
Results may differ from a plain program's by a relative error of at most 0.035.
Values may be sent and summed in bfloat16 or wider, within the bound.
A program may use at most 128 MiB of HBM per device.

v0:
```python
import functools

import jax
import jax.numpy as jnp
from jax import lax
from jax.experimental import pallas as pl
from jax.experimental.pallas import tpu as pltpu
from jax.sharding import PartitionSpec as P

eps = 1e-05
BF = jnp.bfloat16
F32 = jnp.float32
MESH = pl.DeviceIdType.MESH
DOM, SLAB, DEVICES = 8, 16, 128
NODES, EDGES, MIRROR, CAP, L = 512, 8192, 64, 8, 128
CHUNK = 2048
STEPS = EDGES // CHUNK


def mm(a, b):
    return lax.dot_general(a, b, (((1,), (0,)), ((), ())), preferred_element_type=F32)


def mm_nt(a, b):
    return lax.dot_general(a, b, (((1,), (1,)), ((), ())), preferred_element_type=F32)


def averager():
    return jnp.full((L, L), 1.0 / L, BF)


def id_code(row):
    n = row.shape[1]
    low = jnp.broadcast_to((row & 127).astype(F32).astype(BF), (128, n))
    high = jnp.broadcast_to((row >> 7).astype(F32).astype(BF), (128, n))
    place = lax.broadcasted_iota(jnp.int32, (128, n), 0).astype(F32).astype(BF)
    return jnp.where(low == place, high, BF(-1))


def one_hots(code, blocks, axis):
    return jnp.concatenate([jnp.where(code == BF(k), BF(1), BF(0)) for k in range(blocks)], axis)


def halves(x):
    high = x.astype(BF)
    return jnp.concatenate([high, (x - high.astype(F32)).astype(BF)], 1)


def normed(hid, second):
    mixed = mm(hid, second)
    center = mixed - jnp.mean(mixed, 1, keepdims=True)
    rstd = lax.rsqrt(jnp.mean(center * center, 1, keepdims=True) + eps)
    return center * rstd, rstd


def layer(rows, added, first, bias, second):
    pre = mm(jnp.concatenate([rows, added.astype(BF)], 1), first) + bias
    hid = jnp.maximum(pre, 0.0).astype(BF)
    norm, rstd = normed(hid, second)
    return hid, norm, rstd


def layer_back(cot, hid, norm, rstd, first, second, gain):
    scaled = cot * gain
    along = jnp.mean(scaled * norm, 1, keepdims=True)
    cot_mixed = rstd * (scaled - jnp.mean(scaled, 1, keepdims=True) - norm * along)
    cot_hid = mm_nt(cot_mixed.astype(BF), second)
    cot_pre = jnp.where(hid.astype(F32) > 0, cot_hid, 0.0).astype(BF)
    return mm_nt(cot_pre, first)


def edge_forward(snd, rcv, lat, table, mixer, gain, norm_o, hid_o, rstd_o, code_o, sums, write):
    sums[...] = jnp.zeros_like(sums)

    def body(i, carry):
        sl = pl.ds(pl.multiple_of(i * CHUNK, CHUNK), CHUNK)
        s_code, r_code = id_code(snd[:, sl]), id_code(rcv[:, sl])
        s_rows, r_rows = s_code.T, r_code.T
        code_o[sl, :] = r_rows
        rows = lat[sl, :]
        pre = mm(jnp.concatenate([one_hots(s_rows, 6, 1), one_hots(r_rows, 4, 1), rows], 1), table[...])
        hid = jnp.maximum(pre[:, :L] + pre[:, L:], 0.0).astype(BF)
        hid_o[sl, :] = hid
        mixed = mm(hid, mixer)
        center = mixed[:, :L] - mixed[:, L:]
        rstd = lax.rsqrt(mm((center * center).astype(BF), averager()) + eps)
        norm = center * rstd
        norm_o[sl, :] = norm.astype(BF)
        rstd_o[sl, :] = rstd.astype(BF)
        update = norm * gain
        write(i, sl, (rows.astype(F32) + update).astype(BF))
        sums[...] += mm(one_hots(r_code, 4, 0), halves(update))
        return carry

    lax.fori_loop(0, STEPS, body, 0)


def edge_backward(snd, rcv, code_i, cot_table, cot, norm_i, hid_i, rstd_i, w_lat, second, gain, table_o, write):
    table_o[...] = jnp.zeros_like(table_o)

    def body(i, carry):
        sl = pl.ds(pl.multiple_of(i * CHUNK, CHUNK), CHUNK)
        cot_new = cot[sl, :].astype(F32)
        norm = norm_i[sl, :].astype(F32)
        scaled = (cot_new + mm(one_hots(code_i[sl, :], 4, 1), cot_table)) * gain
        along = mm((scaled * norm).astype(BF), averager())
        cot_mixed = (rstd_i[sl, :].astype(F32) * (scaled - norm * along)).astype(BF)
        cot_hid = mm_nt(cot_mixed, second)
        cot_pre = jnp.where(hid_i[sl, :].astype(F32) > 0, cot_hid, 0.0).astype(BF)
        write(i, sl, (cot_new + mm_nt(cot_pre, w_lat)).astype(BF))
        hots = jnp.concatenate([one_hots(id_code(snd[:, sl]), 6, 0), one_hots(id_code(rcv[:, sl]), 4, 0)], 0)
        table_o[...] += mm(hots, cot_pre)
        return carry

    lax.fori_loop(0, STEPS, body, 0)


def kernel(
    snd, rcv, chosen, own_dev, own_slot, lat_h, cot_h, fine, top, cot_fine, cot_top,
    e_first, e_bias, e_second, e_gain, n_first, n_bias, n_second, n_gain, c_first, c_bias, c_second, c_gain,
    new_nodes_o, new_edges_o, new_coarse_o, grad_nodes_o, grad_edges_o, grad_coarse_o,
    lat, cot, norm, hid, rstd, code, new_v, grad_v, table, sums, back_table, pick,
    mir_out, mir_in, early_out, early_in, mid_out, mid_in, grad_out, grad_in, row_out, row_in, ret_out, ret_in,
    load_sem, new_sem, grad_sem, mir_s, mir_r, ret_s, ret_r, early_s, early_r, mid_s, mid_r,
    gback_s, gback_r, row_s, row_r,
):
    dom, slab = lax.axis_index("dom"), lax.axis_index("slab")
    me = dom * SLAB + slab

    load_lat = pltpu.make_async_copy(lat_h, lat, load_sem.at[0])
    load_cot = pltpu.make_async_copy(cot_h, cot, load_sem.at[1])
    load_lat.start()
    load_cot.start()

    def peers(act):
        def body(step, carry):
            other = lax.rem(me + step, DEVICES)
            act(other, (other // SLAB, lax.rem(other, SLAB)))
            return carry

        lax.fori_loop(1, DEVICES, body, 0)

    barrier = pltpu.get_barrier_semaphore()
    peers(lambda other, place: pl.semaphore_signal(barrier, inc=1, device_id=place, device_id_type=MESH))

    def exchange(out, land, send, recv):
        def start(other, place):
            pltpu.make_async_remote_copy(
                src_ref=out.at[other], dst_ref=land.at[me], send_sem=send, recv_sem=recv,
                device_id=place, device_id_type=MESH,
            ).start()

        peers(start)
        land[me] = out[me]

    def finish(out, land, send, recv):
        for ref, sem in ((land, recv), (out, send)):
            whole = ref.at[pl.ds(0, DEVICES - 1)]
            pltpu.make_async_copy(whole, whole, sem).wait()

    def blocks(wide):
        return wide.reshape(DEVICES, CAP, L)

    def rows_of(land):
        return land[...].astype(F32).reshape(DEVICES * CAP, L).astype(BF)

    below, above = (dom - 1, slab), (dom + 1, slab)
    left, right = (dom, slab - 1), (dom, slab + 1)
    has = {"below": dom > 0, "above": dom < DOM - 1, "left": slab > 0, "right": slab < SLAB - 1}
    spot = {"below": below, "above": above, "left": left, "right": right}

    def mirrors(out, land, send, recv, targets, sources):
        copies = [
            pltpu.make_async_remote_copy(
                src_ref=out.at[k], dst_ref=land.at[k], send_sem=send.at[k], recv_sem=recv.at[k],
                device_id=spot[targets[k]], device_id_type=MESH,
            )
            for k in range(4)
        ]
        for k in range(4):
            pl.when(has[targets[k]])(copies[k].start)
            pl.when(jnp.logical_not(has[sources[k]]))(lambda k=k: land.__setitem__(k, jnp.zeros((MIRROR, L), BF)))

        def wait():
            for k in range(4):
                pl.when(has[sources[k]])(copies[k].wait_recv)
                pl.when(has[targets[k]])(copies[k].wait_send)

        return wait

    picked = jnp.concatenate([chosen[k : k + 1, :] for k in range(4)], 1)
    chosen_code = id_code(picked)
    mir_out[...] = mm(one_hots(chosen_code.T, 4, 1), fine[...]).astype(BF).reshape(4, MIRROR, L)

    owner = own_dev[...]
    group = one_hots(id_code(owner), 1, 0)
    place = lax.broadcasted_iota(jnp.int32, (NODES, NODES), 0)
    earlier = jnp.where(place < lax.broadcasted_iota(jnp.int32, (NODES, NODES), 1), 1.0, 0.0).astype(BF)
    rank = jnp.sum(mm(group, earlier) * group.astype(F32), 0, keepdims=True)
    send_code = id_code(owner * CAP + rank.astype(jnp.int32))
    pick[...] = one_hots(send_code, CAP, 0)
    slot_rows = jnp.broadcast_to((own_slot[...] + 1).astype(F32).astype(BF), (L, NODES)).T
    early = mm(pick[...], jnp.concatenate([cot_fine[...], slot_rows], 1))
    early_out[...] = jnp.concatenate([blocks(early[:, :L]), blocks(early[:, L:])], 1).astype(BF)

    pl.semaphore_wait(barrier, DEVICES - 1)
    mirror_wait = mirrors(
        mir_out, mir_in, mir_s, mir_r, ("above", "below", "right", "left"), ("below", "above", "left", "right")
    )
    exchange(early_out, early_in, early_s, early_r)

    w_lat, w_src, w_tgt = e_first[:L, :], e_first[L : 2 * L, :], e_first[2 * L :, :]
    table[:NODES, :] = halves(mm(fine[...], w_src))
    table[6 * L : 10 * L, :] = halves(mm(fine[...], w_tgt) + e_bias[...])
    table[10 * L :, :] = jnp.concatenate([w_lat, jnp.zeros((L, L), BF)], 1)
    second = e_second[...].astype(F32)
    second_mean = jnp.broadcast_to(jnp.mean(second, 1, keepdims=True), (L, L))
    mixer = jnp.concatenate([e_second[...], second_mean.astype(BF)], 1)
    mirror_wait()
    table[NODES : 6 * L, :] = halves(mm(mir_in[...].reshape(4 * MIRROR, L), w_src))
    load_lat.wait()

    def write_new(i, sl, value):
        new_v[sl, :] = value
        pltpu.make_async_copy(new_v.at[sl], new_edges_o.at[sl], new_sem.at[i]).start()

    edge_forward(snd, rcv, lat, table, mixer, e_gain[...], norm, hid, rstd, code, sums, write_new)

    summed = sums[:, :L] + sums[:, L:]
    n_hid, n_norm, n_rstd = layer(fine[...], summed, n_first[...], n_bias[...], n_second[...])
    middle = (fine[...].astype(F32) + n_norm * n_gain[...]).astype(BF)
    mid_out[...] = blocks(mm(pick[...], middle)).astype(BF)
    exchange(mid_out, mid_in, mid_s, mid_r)

    finish(early_out, early_in, early_s, early_r)
    early_rows = early_in[...].astype(F32)
    slots = early_rows[:, CAP:].reshape(DEVICES * CAP, L)
    lane = lax.broadcasted_iota(jnp.int32, (DEVICES * CAP, L), 1).astype(F32)
    held = jnp.where(slots == lane + 1.0, 1.0, 0.0).astype(BF)
    gather = held.T
    cot_at = mm(gather, early_rows[:, :CAP].reshape(DEVICES * CAP, L).astype(BF))
    cot_new = (cot_top[...].astype(F32) + cot_at.astype(BF).astype(F32)).astype(BF).astype(F32)
    finish(mid_out, mid_in, mid_s, mid_r)
    pooled = mm(gather, rows_of(mid_in))
    c_hid, c_norm, c_rstd = layer(top[...], pooled, c_first[...], c_bias[...], c_second[...])
    new_top = (top[...].astype(F32) + c_norm * c_gain[...]).astype(BF)
    c_back = layer_back(cot_new, c_hid, c_norm, c_rstd, c_first[...], c_second[...], c_gain[...])
    grad_out[...] = blocks(mm(held, c_back[:, L:].astype(BF))).astype(BF)
    exchange(grad_out, grad_in, gback_s, gback_r)
    row_out[...] = blocks(mm(held, new_top)).astype(BF)
    exchange(row_out, row_in, row_s, row_r)
    new_coarse_o[...] = new_top
    grad_coarse_o[...] = cot_new + c_back[:, :L]

    second_c = (second - second_mean).astype(BF)
    load_cot.wait()
    finish(grad_out, grad_in, gback_s, gback_r)
    reply = one_hots(send_code.T, CAP, 1)
    cot_mid = (cot_fine[...].astype(F32) + mm(reply, rows_of(grad_in))).astype(BF).astype(F32)
    n_back = layer_back(cot_mid, n_hid, n_norm, n_rstd, n_first[...], n_second[...], n_gain[...])

    def write_grad(i, sl, value):
        grad_v[sl, :] = value
        pltpu.make_async_copy(grad_v.at[sl], grad_edges_o.at[sl], grad_sem.at[i]).start()

    edge_backward(
        snd, rcv, code, n_back[:, L:].astype(BF), cot, norm, hid, rstd, w_lat, second_c, e_gain[...],
        back_table, write_grad,
    )
    back = mm_nt(back_table[NODES : 6 * L, :].astype(BF), w_src)
    ret_out[...] = back.astype(BF).reshape(4, MIRROR, L)
    return_wait = mirrors(
        ret_out, ret_in, ret_s, ret_r, ("below", "above", "left", "right"), ("above", "below", "right", "left")
    )
    total = cot_mid + n_back[:, :L] + mm_nt(back_table[:NODES, :].astype(BF), w_src)
    total = total + mm_nt(back_table[6 * L :, :].astype(BF), w_tgt)
    finish(row_out, row_in, row_s, row_r)
    new_nodes_o[...] = (middle.astype(F32) + mm(reply, rows_of(row_in))).astype(BF)
    return_wait()
    grad_nodes_o[...] = total + mm(one_hots(chosen_code, 4, 0), ret_in[...].reshape(4 * MIRROR, L))
    for i in range(STEPS):
        sl = pl.ds(i * CHUNK, CHUNK)
        pltpu.make_async_copy(new_v.at[sl], new_edges_o.at[sl], new_sem.at[i]).wait()
        pltpu.make_async_copy(grad_v.at[sl], grad_edges_o.at[sl], grad_sem.at[i]).wait()


VM = pl.BlockSpec(memory_space=pltpu.VMEM)
ANY = pl.BlockSpec(memory_space=pl.ANY)


def shaped(*sizes, dtype=BF):
    return jax.ShapeDtypeStruct(sizes, dtype)


def local(
    nodes, edges, coarse, senders, receivers, mirror_rows, owner_device, owner_slot,
    edge_first, edge_bias, edge_second, edge_gain, node_first, node_bias, node_second, node_gain,
    coarse_first, coarse_bias, coarse_second, coarse_gain, cot_nodes, cot_edges, cot_coarse,
):
    def line(v):
        return v.reshape(1, -1)

    edge_rows = [pltpu.VMEM((EDGES, L), BF)] * 8
    pair = lambda *sizes: [pltpu.VMEM(sizes, BF)] * 2
    dma = pltpu.SemaphoreType.DMA
    outs = pl.pallas_call(
        kernel,
        out_shape=[
            shaped(NODES, L), shaped(EDGES, L), shaped(128, L),
            shaped(NODES, L, dtype=F32), shaped(EDGES, L), shaped(128, L, dtype=F32),
        ],
        in_specs=[VM] * 5 + [ANY] * 2 + [VM] * 16,
        out_specs=[VM, ANY, VM, VM, ANY, VM],
        scratch_shapes=edge_rows
        + [
            pltpu.VMEM((11 * L, 2 * L), BF), pltpu.VMEM((NODES, 2 * L), F32), pltpu.VMEM((10 * L, L), F32),
            pltpu.VMEM((DEVICES * CAP, NODES), BF),
        ]
        + pair(4, MIRROR, L) + pair(DEVICES, 2 * CAP, L) + pair(DEVICES, CAP, L) * 3 + pair(4, MIRROR, L)
        + [dma((2,)), dma((STEPS,)), dma((STEPS,))] + [dma((4,))] * 4 + [dma] * 8,
        compiler_params=pltpu.CompilerParams(
            vmem_limit_bytes=58 << 20, collective_id=0, has_side_effects=True
        ),
        name="mesh_layer",
    )(
        line(senders), line(receivers), mirror_rows[0, 0], line(owner_device), line(owner_slot),
        edges[0, 0], cot_edges[0, 0], nodes[0, 0], coarse[0, 0], cot_nodes[0, 0], cot_coarse[0, 0],
        edge_first, line(edge_bias), edge_second, line(edge_gain),
        node_first, line(node_bias), node_second, line(node_gain),
        coarse_first, line(coarse_bias), coarse_second, line(coarse_gain),
    )
    outs = list(outs)
    outs[4] = outs[4].astype(F32)
    return tuple(o[None, None] for o in outs)


def solution(mesh):
    four, three, whole = P("dom", "slab", None, None), P("dom", "slab", None), P()
    in_specs = (four, four, four, three, three, four, four, three) + (whole,) * 12 + (four,) * 3
    return jax.shard_map(local, mesh=mesh, in_specs=in_specs, out_specs=(four,) * 6, check_vma=False)
```

profile of v0, /device:TPU:1, one launch (start us, length us, event | category | flops | bytes accessed | tf_op | source)
XLA Modules:
  0.0 76.1 jit_solution(8689714800680269007)
XLA Ops:
  0.6 67.5 %mesh_layer.1 = (bf16[512,128]{1,0:T(8,128)(2,1)}, bf16[8192,128]{1,0:T(8,128)(2,1)}, bf16[128,128]{1,0:T(8,128)(2,1)}, f32[512,128]{1,0:T(8,128)}, bf16[8192,128]{1,0:T(8,128)(2,1)}, /*index=5*/f32[128,128]{1,0:T(8,128)}) custom-call(s32[1,8192]{1,0:T(1,128)} %bitcast.33, s32[1,8192]{1,0:T(1,128)} %bitcast.34, s32[4,64]{1,0:T(4,128)} %bitcast.38, ...), custom_call_target="tpu_custom_call" | custom-call | tf_op jit(solution)/shard_map/mesh_layer/pallas_call | solution.py:306
  68.1 0.0 copy-start.2
  68.1 0.0 copy-start
  68.1 4.0 %bitcast_convert_fusion = f32[1,1,8192,128]{3,2,1,0:T(8,128)} fusion(bf16[8192,128]{1,0:T(8,128)(2,1)} %get-tuple-element.16), kind=kLoop, calls=%fused_computation | loop fusion | flops 1048576 | bytes 6291456 | tf_op jit(solution)/shard_map/broadcast_in_dim | solution.py:334
  72.2 0.0 copy-done.2
  72.2 0.7 copy.34
  72.8 0.0 copy-done
  72.8 0.0 copy-start.4
  72.8 0.0 copy-start.1
  72.8 0.0 copy-start.3
  72.8 1.3 %copy.35 = bf16[1,1,8192,128]{3,2,1,0:T(8,128)(2,1)} copy(bf16[1,1,8192,128]{3,2,1,0:T(8,128)(2,1)S(1)} %bitcast.25) | data formatting | bytes 4194304
  74.2 0.0 copy-done.4
  74.2 0.6 copy.36
  74.8 0.0 copy-done.1
  74.8 0.7 copy.37
  75.5 0.0 copy-done.3
  75.5 0.6 copy.38
Async XLA Ops:
  68.1 4.0 %copy-start.2 = (bf16[512,128]{1,0:T(8,128)(2,1)S(1)}, bf16[512,128]{1,0:T(8,128)(2,1)}, u32[]{:S(2)}) copy-start(bf16[512,128]{1,0:T(8,128)(2,1)} %get-tuple-element.12) | copy-start | bytes 393220
  68.1 4.7 %copy-start = (bf16[8192,128]{1,0:T(8,128)(2,1)S(1)}, bf16[8192,128]{1,0:T(8,128)(2,1)}, u32[]{:S(2)}) copy-start(bf16[8192,128]{1,0:T(8,128)(2,1)} %get-tuple-element.13) | copy-start | bytes 6291460
  72.8 1.3 %copy-start.4 = (bf16[128,128]{1,0:T(8,128)(2,1)S(1)}, bf16[128,128]{1,0:T(8,128)(2,1)}, u32[]{:S(2)}) copy-start(bf16[128,128]{1,0:T(8,128)(2,1)} %get-tuple-element.14) | copy-start | bytes 98308
  72.8 1.9 %copy-start.1 = (f32[512,128]{1,0:T(8,128)S(1)}, f32[512,128]{1,0:T(8,128)}, u32[]{:S(2)}) copy-start(f32[512,128]{1,0:T(8,128)} %get-tuple-element.15) | copy-start | bytes 786436
  72.8 2.7 %copy-start.3 = (f32[128,128]{1,0:T(8,128)S(1)}, f32[128,128]{1,0:T(8,128)}, u32[]{:S(2)}) copy-start(f32[128,128]{1,0:T(8,128)} %get-tuple-element.17) | copy-start | bytes 196612
where the time goes:
time: 76.2 us; the launch traced here: 76.1 us
  Pallas kernels  67.5 us (89%)
  other arithmetic  4.03 us (5%)
  local copies, waits for them, and re-layouts  3.94 us (5%)
    pallas_call x1, Pallas kernels, local(): pl.pallas_call(kernel, out_shape=[shaped(NODES, L), shaped(EDGES, L), sha...  67.5 us
    broadcast_in_dim x1, other arithmetic, local(): return tuple((o[None, None] for o in outs))  4.03 us
    unnamed x15, local copies, waits for them, and re-layouts  3.94 us

commit v1 on v0

--- a/solution.py
+++ b/solution.py
@@ -15,6 +15,8 @@
 NODES, EDGES, MIRROR, CAP, L = 512, 8192, 64, 8, 128
 CHUNK = 2048
 STEPS = EDGES // CHUNK
+PARTS = 4
+INPUTS = 23
 
 
 def mm(a, b):
@@ -69,68 +71,92 @@
     return mm_nt(cot_pre, first)
 
 
-def edge_forward(snd, rcv, lat, table, mixer, gain, norm_o, hid_o, rstd_o, code_o, sums, write):
+def staged(first, second, between=None):
+    first(0)
+
+    def body(i, carry):
+        if between is not None:
+            between(i - 1)
+        second(i - 1)
+        first(i)
+        return carry
+
+    lax.fori_loop(1, STEPS, body, 0)
+    second(STEPS - 1)
+
+
+def rows_at(i):
+    return pl.ds(i * CHUNK if isinstance(i, int) else pl.multiple_of(i * CHUNK, CHUNK), CHUNK)
+
+
+def edge_forward(snd, rcv, lat, table, mixer, gain, norm_o, hid_o, rstd_o, code_o, sums, write, between):
     sums[...] = jnp.zeros_like(sums)
 
-    def body(i, carry):
-        sl = pl.ds(pl.multiple_of(i * CHUNK, CHUNK), CHUNK)
-        s_code, r_code = id_code(snd[:, sl]), id_code(rcv[:, sl])
-        s_rows, r_rows = s_code.T, r_code.T
+    def gather(i):
+        sl = rows_at(i)
+        s_rows, r_rows = id_code(snd[:, sl]).T, id_code(rcv[:, sl]).T
         code_o[sl, :] = r_rows
-        rows = lat[sl, :]
-        pre = mm(jnp.concatenate([one_hots(s_rows, 6, 1), one_hots(r_rows, 4, 1), rows], 1), table[...])
-        hid = jnp.maximum(pre[:, :L] + pre[:, L:], 0.0).astype(BF)
-        hid_o[sl, :] = hid
-        mixed = mm(hid, mixer)
+        pre = mm(jnp.concatenate([one_hots(s_rows, 6, 1), one_hots(r_rows, 4, 1), lat[sl, :]], 1), table[...])
+        hid_o[sl, :] = jnp.maximum(pre[:, :L] + pre[:, L:], 0.0).astype(BF)
+
+    def update(i):
+        sl = rows_at(i)
+        mixed = mm(hid_o[sl, :], mixer)
         center = mixed[:, :L] - mixed[:, L:]
         rstd = lax.rsqrt(mm((center * center).astype(BF), averager()) + eps)
         norm = center * rstd
         norm_o[sl, :] = norm.astype(BF)
         rstd_o[sl, :] = rstd.astype(BF)
-        update = norm * gain
-        write(i, sl, (rows.astype(F32) + update).astype(BF))
-        sums[...] += mm(one_hots(r_code, 4, 0), halves(update))
-        return carry
-
-    lax.fori_loop(0, STEPS, body, 0)
-
-
-def edge_backward(snd, rcv, code_i, cot_table, cot, norm_i, hid_i, rstd_i, w_lat, second, gain, table_o, write):
+        change = norm * gain
+        write(i, sl, (lat[sl, :].astype(F32) + change).astype(BF))
+        sums[...] += mm(one_hots(id_code(rcv[:, sl]), 4, 0), halves(change))
+
+    staged(gather, update, between)
+
+
+def edge_backward(
+    snd, rcv, code_i, cot_table, cot, norm_i, hid_i, rstd_i, w_lat, second, gain, table_o, pre_o, write
+):
     table_o[...] = jnp.zeros_like(table_o)
 
-    def body(i, carry):
-        sl = pl.ds(pl.multiple_of(i * CHUNK, CHUNK), CHUNK)
-        cot_new = cot[sl, :].astype(F32)
+    def through(i):
+        sl = rows_at(i)
         norm = norm_i[sl, :].astype(F32)
-        scaled = (cot_new + mm(one_hots(code_i[sl, :], 4, 1), cot_table)) * gain
+        scaled = (cot[sl, :].astype(F32) + mm(one_hots(code_i[sl, :], 4, 1), cot_table)) * gain
         along = mm((scaled * norm).astype(BF), averager())
         cot_mixed = (rstd_i[sl, :].astype(F32) * (scaled - norm * along)).astype(BF)
         cot_hid = mm_nt(cot_mixed, second)
-        cot_pre = jnp.where(hid_i[sl, :].astype(F32) > 0, cot_hid, 0.0).astype(BF)
-        write(i, sl, (cot_new + mm_nt(cot_pre, w_lat)).astype(BF))
+        pre_o[sl, :] = jnp.where(hid_i[sl, :].astype(F32) > 0, cot_hid, 0.0).astype(BF)
+
+    def spread(i):
+        sl = rows_at(i)
+        cot_pre = pre_o[sl, :]
+        write(i, sl, (cot[sl, :].astype(F32) + mm_nt(cot_pre, w_lat)).astype(BF))
         hots = jnp.concatenate([one_hots(id_code(snd[:, sl]), 6, 0), one_hots(id_code(rcv[:, sl]), 4, 0)], 0)
         table_o[...] += mm(hots, cot_pre)
-        return carry
-
-    lax.fori_loop(0, STEPS, body, 0)
-
-
-def kernel(
-    snd, rcv, chosen, own_dev, own_slot, lat_h, cot_h, fine, top, cot_fine, cot_top,
-    e_first, e_bias, e_second, e_gain, n_first, n_bias, n_second, n_gain, c_first, c_bias, c_second, c_gain,
-    new_nodes_o, new_edges_o, new_coarse_o, grad_nodes_o, grad_edges_o, grad_coarse_o,
-    lat, cot, norm, hid, rstd, code, new_v, grad_v, table, sums, back_table, pick,
-    mir_out, mir_in, early_out, early_in, mid_out, mid_in, grad_out, grad_in, row_out, row_in, ret_out, ret_in,
-    load_sem, new_sem, grad_sem, mir_s, mir_r, ret_s, ret_r, early_s, early_r, mid_s, mid_r,
-    gback_s, gback_r, row_s, row_r,
-):
+
+    staged(through, spread)
+
+
+def kernel(*refs):
+    sources, targets, rest = refs[:INPUTS], refs[INPUTS + 6 : 2 * INPUTS + 6], refs[2 * INPUTS + 6 :]
+    (
+        snd, rcv, chosen, own_dev, own_slot, lat, cot, fine, top, cot_fine, cot_top,
+        e_first, e_bias, e_second, e_gain, n_first, n_bias, n_second, n_gain, c_first, c_bias, c_second, c_gain,
+    ) = targets
+    new_nodes_o, new_edges_o, new_coarse_o, grad_nodes_o, grad_edges_o, grad_coarse_o = refs[INPUTS : INPUTS + 6]
+    (
+        norm, hid, rstd, code, new_v, grad_v, cot_pre, table, sums, back_table, pick,
+        mir_out, mir_in, early_out, early_in, mid_out, mid_in, grad_out, grad_in, row_out, row_in, ret_out, ret_in,
+        load_sem, new_sem, grad_sem, mir_s, mir_r, ret_s, ret_r, early_s, early_r, mid_s, mid_r,
+        gback_s, gback_r, row_s, row_r,
+    ) = rest
     dom, slab = lax.axis_index("dom"), lax.axis_index("slab")
     me = dom * SLAB + slab
 
-    load_lat = pltpu.make_async_copy(lat_h, lat, load_sem.at[0])
-    load_cot = pltpu.make_async_copy(cot_h, cot, load_sem.at[1])
-    load_lat.start()
-    load_cot.start()
+    loads = [pltpu.make_async_copy(src, dst, load_sem.at[k]) for k, (src, dst) in enumerate(zip(sources, targets))]
+    for load in loads:
+        load.start()
 
     def peers(act):
         def body(step, carry):
@@ -188,6 +214,10 @@
 
         return wait
 
+    for k, load in enumerate(loads):
+        if k not in (5, 6):
+            load.wait()
+
     picked = jnp.concatenate([chosen[k : k + 1, :] for k in range(4)], 1)
     chosen_code = id_code(picked)
     mir_out[...] = mm(one_hots(chosen_code.T, 4, 1), fine[...]).astype(BF).reshape(4, MIRROR, L)
@@ -218,13 +248,13 @@
     mixer = jnp.concatenate([e_second[...], second_mean.astype(BF)], 1)
     mirror_wait()
     table[NODES : 6 * L, :] = halves(mm(mir_in[...].reshape(4 * MIRROR, L), w_src))
-    load_lat.wait()
+    loads[5].wait()
 
     def write_new(i, sl, value):
         new_v[sl, :] = value
         pltpu.make_async_copy(new_v.at[sl], new_edges_o.at[sl], new_sem.at[i]).start()
 
-    edge_forward(snd, rcv, lat, table, mixer, e_gain[...], norm, hid, rstd, code, sums, write_new)
+    edge_forward(snd, rcv, lat, table, mixer, e_gain[...], norm, hid, rstd, code, sums, write_new, None)
 
     summed = sums[:, :L] + sums[:, L:]
     n_hid, n_norm, n_rstd = layer(fine[...], summed, n_first[...], n_bias[...], n_second[...])
@@ -253,7 +283,7 @@
     grad_coarse_o[...] = cot_new + c_back[:, :L]
 
     second_c = (second - second_mean).astype(BF)
-    load_cot.wait()
+    loads[6].wait()
     finish(grad_out, grad_in, gback_s, gback_r)
     reply = one_hots(send_code.T, CAP, 1)
     cot_mid = (cot_fine[...].astype(F32) + mm(reply, rows_of(grad_in))).astype(BF).astype(F32)
@@ -265,7 +295,7 @@
 
     edge_backward(
         snd, rcv, code, n_back[:, L:].astype(BF), cot, norm, hid, rstd, w_lat, second_c, e_gain[...],
-        back_table, write_grad,
+        back_table, cot_pre, write_grad,
     )
     back = mm_nt(back_table[NODES : 6 * L, :].astype(BF), w_src)
     ret_out[...] = back.astype(BF).reshape(4, MIRROR, L)
@@ -284,7 +314,34 @@
         pltpu.make_async_copy(grad_v.at[sl], grad_edges_o.at[sl], grad_sem.at[i]).wait()
 
 
+def finish_kernel(*refs):
+    ins, outs, held, (wide, load_sems, sems) = refs[:6], refs[6:12], refs[12:18], refs[18:]
+    work = []
+    for k in (4, 1, 0, 3, 2, 5):
+        rows = ins[k].shape[0]
+        count = PARTS if rows == EDGES else 1
+        for i in range(count):
+            sl = pl.ds(i * (rows // count), rows // count)
+            n = len(work)
+            final = wide if k == 4 else held[k]
+            work.append((
+                k, sl,
+                pltpu.make_async_copy(ins[k].at[sl], held[k].at[sl], load_sems.at[n]),
+                pltpu.make_async_copy(final.at[sl], outs[k].at[sl], sems.at[n]),
+            ))
+    for k, sl, load, store in work:
+        load.start()
+    for k, sl, load, store in work:
+        load.wait()
+        if k == 4:
+            wide[sl, :] = held[k][sl, :].astype(F32)
+        store.start()
+    for k, sl, load, store in work:
+        store.wait()
+
+
 VM = pl.BlockSpec(memory_space=pltpu.VMEM)
+HBM = pl.BlockSpec(memory_space=pltpu.HBM)
 ANY = pl.BlockSpec(memory_space=pl.ANY)
 
 
@@ -300,37 +357,50 @@
     def line(v):
         return v.reshape(1, -1)
 
-    edge_rows = [pltpu.VMEM((EDGES, L), BF)] * 8
+    edge_rows = [pltpu.VMEM((EDGES, L), BF)] * 7
     pair = lambda *sizes: [pltpu.VMEM(sizes, BF)] * 2
     dma = pltpu.SemaphoreType.DMA
+    ins = (
+        line(senders), line(receivers), mirror_rows[0, 0], line(owner_device), line(owner_slot),
+        edges[0, 0], cot_edges[0, 0], nodes[0, 0], coarse[0, 0], cot_nodes[0, 0], cot_coarse[0, 0],
+        edge_first, line(edge_bias), edge_second, line(edge_gain),
+        node_first, line(node_bias), node_second, line(node_gain),
+        coarse_first, line(coarse_bias), coarse_second, line(coarse_gain),
+    )
     outs = pl.pallas_call(
         kernel,
         out_shape=[
             shaped(NODES, L), shaped(EDGES, L), shaped(128, L),
             shaped(NODES, L, dtype=F32), shaped(EDGES, L), shaped(128, L, dtype=F32),
         ],
-        in_specs=[VM] * 5 + [ANY] * 2 + [VM] * 16,
-        out_specs=[VM, ANY, VM, VM, ANY, VM],
-        scratch_shapes=edge_rows
+        in_specs=[HBM] * INPUTS,
+        out_specs=[VM, HBM, VM, VM, HBM, VM],
+        scratch_shapes=[pltpu.VMEM(v.shape, v.dtype) for v in ins]
+        + edge_rows
         + [
             pltpu.VMEM((11 * L, 2 * L), BF), pltpu.VMEM((NODES, 2 * L), F32), pltpu.VMEM((10 * L, L), F32),
             pltpu.VMEM((DEVICES * CAP, NODES), BF),
         ]
         + pair(4, MIRROR, L) + pair(DEVICES, 2 * CAP, L) + pair(DEVICES, CAP, L) * 3 + pair(4, MIRROR, L)
-        + [dma((2,)), dma((STEPS,)), dma((STEPS,))] + [dma((4,))] * 4 + [dma] * 8,
+        + [dma((INPUTS,)), dma((STEPS,)), dma((STEPS,))] + [dma((4,))] * 4 + [dma] * 8,
         compiler_params=pltpu.CompilerParams(
             vmem_limit_bytes=58 << 20, collective_id=0, has_side_effects=True
         ),
         name="mesh_layer",
-    )(
-        line(senders), line(receivers), mirror_rows[0, 0], line(owner_device), line(owner_slot),
-        edges[0, 0], cot_edges[0, 0], nodes[0, 0], coarse[0, 0], cot_nodes[0, 0], cot_coarse[0, 0],
-        edge_first, line(edge_bias), edge_second, line(edge_gain),
-        node_first, line(node_bias), node_second, line(node_gain),
-        coarse_first, line(coarse_bias), coarse_second, line(coarse_gain),
-    )
-    outs = list(outs)
-    outs[4] = outs[4].astype(F32)
+    )(*ins)
+    outs = pl.pallas_call(
+        finish_kernel,
+        out_shape=[
+            shaped(NODES, L), shaped(EDGES, L), shaped(128, L),
+            shaped(NODES, L, dtype=F32), shaped(EDGES, L, dtype=F32), shaped(128, L, dtype=F32),
+        ],
+        in_specs=[HBM] * 6,
+        out_specs=[HBM] * 6,
+        scratch_shapes=[pltpu.VMEM(v.shape, v.dtype) for v in outs]
+        + [pltpu.VMEM((EDGES, L), F32)] + [dma((2 * PARTS + 4,))] * 2,
+        compiler_params=pltpu.CompilerParams(vmem_limit_bytes=58 << 20),
+        name="write_results",
+    )(*outs)
     return tuple(o[None, None] for o in outs)
 
 

time: 76.2 us -> 67.2 us (0.88)
  other arithmetic: 4.03 us -> 0 us
  local copies, waits for them, and re-layouts: 3.94 us -> 0 us
  Pallas kernels: 67.5 us -> 66.3 us
    pallas_call x1, Pallas kernels: 67.5 us -> 62.2 us  [local(): pl.pallas_call(kernel, out_shape=[shaped(NODES, L), shaped(EDGES, L), sha...]
    pallas_call x0 -> x1, Pallas kernels: none -> 4.09 us  [local(): pl.pallas_call(finish_kernel, out_shape=[shaped(NODES, L), shaped(EDGES,...]
    broadcast_in_dim x1 -> x0, other arithmetic: 4.03 us -> none  [local(): return tuple((o[None, None] for o in outs))]
    unnamed x15 -> x0, local copies, waits for them, and re-layouts: 3.94 us -> none
where the time goes in v1:
time: 67.2 us; the launch traced here: 67.1 us
  Pallas kernels  66.3 us (99%)
  between operations  0.81 us (1%)
    pallas_call x1, Pallas kernels, local(): pl.pallas_call(kernel, out_shape=[shaped(NODES, L), shaped(EDGES, L), sha...  62.2 us
    pallas_call x1, Pallas kernels, local(): pl.pallas_call(finish_kernel, out_shape=[shaped(NODES, L), shaped(EDGES,...  4.09 us

profile of v1, /device:TPU:1, one launch (start us, length us, event | category | flops | bytes accessed | tf_op | source)
XLA Modules:
  0.0 67.1 jit_solution(15693130928829523594)
XLA Ops:
  0.6 62.2 %mesh_layer.1 = (bf16[512,128]{1,0:T(8,128)(2,1)}, bf16[8192,128]{1,0:T(8,128)(2,1)}, bf16[128,128]{1,0:T(8,128)(2,1)}, f32[512,128]{1,0:T(8,128)}, bf16[8192,128]{1,0:T(8,128)(2,1)}, /*index=5*/f32[128,128]{1,0:T(8,128)}) custom-call(s32[1,8192]{1,0:T(1,128)} %bitcast.27, s32[1,8192]{1,0:T(1,128)} %bitcast.28, s32[4,64]{1,0:T(4,128)} %bitcast.31, ...), custom_call_target="tpu_custom_call" | custom-call | tf_op jit(solution)/shard_map/mesh_layer/pallas_call | solution.py:370
  62.8 4.1 %write_results.1 = (bf16[512,128]{1,0:T(8,128)(2,1)}, bf16[8192,128]{1,0:T(8,128)(2,1)}, bf16[128,128]{1,0:T(8,128)(2,1)}, f32[512,128]{1,0:T(8,128)}, f32[8192,128]{1,0:T(8,128)}, /*index=5*/f32[128,128]{1,0:T(8,128)}) custom-call(bf16[512,128]{1,0:T(8,128)(2,1)} %get-tuple-element.18.refs_0_, bf16[8192,128]{1,0:T(8,128)(2,1)} %get-tuple-element.19.refs_1_, ...), custom_call_target="tpu_custom_call" | custom-call | tf_op jit(solution)/shard_map/write_results/pallas_call | solution.py:391

commit v2 on v1

--- a/solution.py
+++ b/solution.py
@@ -17,6 +17,9 @@
 STEPS = EDGES // CHUNK
 PARTS = 4
 INPUTS = 23
+FIRST = (7, 2, 3, 4, 9)
+LAST = (5, 6)
+S_HALF, R_HALF = 384, 256
 
 
 def mm(a, b):
@@ -89,13 +92,12 @@
     return pl.ds(i * CHUNK if isinstance(i, int) else pl.multiple_of(i * CHUNK, CHUNK), CHUNK)
 
 
-def edge_forward(snd, rcv, lat, table, mixer, gain, norm_o, hid_o, rstd_o, code_o, sums, write, between):
+def edge_forward(snd, rcv, lat, table, mixer, gain, norm_o, hid_o, rstd_o, sums, write, between):
     sums[...] = jnp.zeros_like(sums)
 
     def gather(i):
         sl = rows_at(i)
         s_rows, r_rows = id_code(snd[:, sl]).T, id_code(rcv[:, sl]).T
-        code_o[sl, :] = r_rows
         pre = mm(jnp.concatenate([one_hots(s_rows, 6, 1), one_hots(r_rows, 4, 1), lat[sl, :]], 1), table[...])
         hid_o[sl, :] = jnp.maximum(pre[:, :L] + pre[:, L:], 0.0).astype(BF)
 
@@ -103,10 +105,10 @@
         sl = rows_at(i)
         mixed = mm(hid_o[sl, :], mixer)
         center = mixed[:, :L] - mixed[:, L:]
-        rstd = lax.rsqrt(mm((center * center).astype(BF), averager()) + eps)
+        rstd = lax.rsqrt(jnp.mean(center * center, 1, keepdims=True) + eps)
         norm = center * rstd
         norm_o[sl, :] = norm.astype(BF)
-        rstd_o[sl, :] = rstd.astype(BF)
+        rstd_o[sl, :] = jnp.broadcast_to(rstd, norm.shape).astype(BF)
         change = norm * gain
         write(i, sl, (lat[sl, :].astype(F32) + change).astype(BF))
         sums[...] += mm(one_hots(id_code(rcv[:, sl]), 4, 0), halves(change))
@@ -114,15 +116,49 @@
     staged(gather, update, between)
 
 
+def edge_prepare(snd, rcv, code_o, s_upper, r_upper):
+    def body(i, carry):
+        sl = rows_at(i)
+        for ids, half, upper in ((snd, S_HALF, s_upper), (rcv, R_HALF, r_upper)):
+            flag = jnp.where(ids[:, sl] >= half, 1.0, 0.0).astype(BF)
+            upper[sl, :] = jnp.broadcast_to(flag, (L, CHUNK)).T
+        code_o[sl, :] = id_code(within(rcv[:, sl], R_HALF)).T
+        return carry
+
+    lax.fori_loop(0, STEPS, body, 0)
+
+
+def within(ids, half):
+    return jnp.where(ids >= half, ids - half, ids)
+
+
+def beside(rows):
+    half = rows.shape[0] // 2
+    return jnp.concatenate([rows[:half], rows[half:]], 1)
+
+
+def below_each_other(pair):
+    return jnp.concatenate([pair[:, :L], pair[:, L:]], 0)
+
+
+def parted(rows, upper):
+    chosen = upper > BF(0)
+    return jnp.concatenate([jnp.where(chosen, BF(0), rows), jnp.where(chosen, rows, BF(0))], 1)
+
+
 def edge_backward(
-    snd, rcv, code_i, cot_table, cot, norm_i, hid_i, rstd_i, w_lat, second, gain, table_o, pre_o, write
+    snd, rcv, code_i, s_upper, r_upper, cot_table, cot, norm_i, hid_i, rstd_i, w_lat, second, gain,
+    s_table, r_table, pre_o, write,
 ):
-    table_o[...] = jnp.zeros_like(table_o)
+    s_table[...] = jnp.zeros_like(s_table)
+    r_table[...] = jnp.zeros_like(r_table)
 
     def through(i):
         sl = rows_at(i)
         norm = norm_i[sl, :].astype(F32)
-        scaled = (cot[sl, :].astype(F32) + mm(one_hots(code_i[sl, :], 4, 1), cot_table)) * gain
+        found = mm(one_hots(code_i[sl, :], 2, 1), cot_table)
+        found = jnp.where(r_upper[sl, :].astype(F32) > 0, found[:, L:], found[:, :L])
+        scaled = (cot[sl, :].astype(F32) + found) * gain
         along = mm((scaled * norm).astype(BF), averager())
         cot_mixed = (rstd_i[sl, :].astype(F32) * (scaled - norm * along)).astype(BF)
         cot_hid = mm_nt(cot_mixed, second)
@@ -132,8 +168,9 @@
         sl = rows_at(i)
         cot_pre = pre_o[sl, :]
         write(i, sl, (cot[sl, :].astype(F32) + mm_nt(cot_pre, w_lat)).astype(BF))
-        hots = jnp.concatenate([one_hots(id_code(snd[:, sl]), 6, 0), one_hots(id_code(rcv[:, sl]), 4, 0)], 0)
-        table_o[...] += mm(hots, cot_pre)
+        s_code, r_code = id_code(within(snd[:, sl], S_HALF)), id_code(within(rcv[:, sl], R_HALF))
+        s_table[...] += mm(one_hots(s_code, 3, 0), parted(cot_pre, s_upper[sl, :]))
+        r_table[...] += mm(one_hots(r_code, 2, 0), parted(cot_pre, r_upper[sl, :]))
 
     staged(through, spread)
 
@@ -146,7 +183,7 @@
     ) = targets
     new_nodes_o, new_edges_o, new_coarse_o, grad_nodes_o, grad_edges_o, grad_coarse_o = refs[INPUTS : INPUTS + 6]
     (
-        norm, hid, rstd, code, new_v, grad_v, cot_pre, table, sums, back_table, pick,
+        norm, hid, rstd, code, new_v, grad_v, cot_pre, s_upper, r_upper, table, sums, s_table, r_table, pick,
         mir_out, mir_in, early_out, early_in, mid_out, mid_in, grad_out, grad_in, row_out, row_in, ret_out, ret_in,
         load_sem, new_sem, grad_sem, mir_s, mir_r, ret_s, ret_r, early_s, early_r, mid_s, mid_r,
         gback_s, gback_r, row_s, row_r,
@@ -155,8 +192,8 @@
     me = dom * SLAB + slab
 
     loads = [pltpu.make_async_copy(src, dst, load_sem.at[k]) for k, (src, dst) in enumerate(zip(sources, targets))]
-    for load in loads:
-        load.start()
+    for k in FIRST + tuple(k for k in range(INPUTS) if k not in FIRST + LAST) + LAST:
+        loads[k].start()
 
     def peers(act):
         def body(step, carry):
@@ -222,6 +259,11 @@
     chosen_code = id_code(picked)
     mir_out[...] = mm(one_hots(chosen_code.T, 4, 1), fine[...]).astype(BF).reshape(4, MIRROR, L)
 
+    pl.semaphore_wait(barrier, DEVICES - 1)
+    mirror_wait = mirrors(
+        mir_out, mir_in, mir_s, mir_r, ("above", "below", "right", "left"), ("below", "above", "left", "right")
+    )
+
     owner = own_dev[...]
     group = one_hots(id_code(owner), 1, 0)
     place = lax.broadcasted_iota(jnp.int32, (NODES, NODES), 0)
@@ -232,11 +274,6 @@
     slot_rows = jnp.broadcast_to((own_slot[...] + 1).astype(F32).astype(BF), (L, NODES)).T
     early = mm(pick[...], jnp.concatenate([cot_fine[...], slot_rows], 1))
     early_out[...] = jnp.concatenate([blocks(early[:, :L]), blocks(early[:, L:])], 1).astype(BF)
-
-    pl.semaphore_wait(barrier, DEVICES - 1)
-    mirror_wait = mirrors(
-        mir_out, mir_in, mir_s, mir_r, ("above", "below", "right", "left"), ("below", "above", "left", "right")
-    )
     exchange(early_out, early_in, early_s, early_r)
 
     w_lat, w_src, w_tgt = e_first[:L, :], e_first[L : 2 * L, :], e_first[2 * L :, :]
@@ -254,13 +291,14 @@
         new_v[sl, :] = value
         pltpu.make_async_copy(new_v.at[sl], new_edges_o.at[sl], new_sem.at[i]).start()
 
-    edge_forward(snd, rcv, lat, table, mixer, e_gain[...], norm, hid, rstd, code, sums, write_new, None)
+    edge_forward(snd, rcv, lat, table, mixer, e_gain[...], norm, hid, rstd, sums, write_new, None)
 
     summed = sums[:, :L] + sums[:, L:]
     n_hid, n_norm, n_rstd = layer(fine[...], summed, n_first[...], n_bias[...], n_second[...])
     middle = (fine[...].astype(F32) + n_norm * n_gain[...]).astype(BF)
     mid_out[...] = blocks(mm(pick[...], middle)).astype(BF)
     exchange(mid_out, mid_in, mid_s, mid_r)
+    edge_prepare(snd, rcv, code, s_upper, r_upper)
 
     finish(early_out, early_in, early_s, early_r)
     early_rows = early_in[...].astype(F32)
@@ -294,16 +332,17 @@
         pltpu.make_async_copy(grad_v.at[sl], grad_edges_o.at[sl], grad_sem.at[i]).start()
 
     edge_backward(
-        snd, rcv, code, n_back[:, L:].astype(BF), cot, norm, hid, rstd, w_lat, second_c, e_gain[...],
-        back_table, cot_pre, write_grad,
+        snd, rcv, code, s_upper, r_upper, beside(n_back[:, L:].astype(BF)), cot, norm, hid, rstd,
+        w_lat, second_c, e_gain[...], s_table, r_table, cot_pre, write_grad,
     )
-    back = mm_nt(back_table[NODES : 6 * L, :].astype(BF), w_src)
+    back_table = below_each_other(s_table[...]).astype(BF)
+    back = mm_nt(back_table[NODES:], w_src)
     ret_out[...] = back.astype(BF).reshape(4, MIRROR, L)
     return_wait = mirrors(
         ret_out, ret_in, ret_s, ret_r, ("below", "above", "left", "right"), ("above", "below", "right", "left")
     )
-    total = cot_mid + n_back[:, :L] + mm_nt(back_table[:NODES, :].astype(BF), w_src)
-    total = total + mm_nt(back_table[6 * L :, :].astype(BF), w_tgt)
+    total = cot_mid + n_back[:, :L] + mm_nt(back_table[:NODES], w_src)
+    total = total + mm_nt(below_each_other(r_table[...]).astype(BF), w_tgt)
     finish(row_out, row_in, row_s, row_r)
     new_nodes_o[...] = (middle.astype(F32) + mm(reply, rows_of(row_in))).astype(BF)
     return_wait()
@@ -357,7 +396,7 @@
     def line(v):
         return v.reshape(1, -1)
 
-    edge_rows = [pltpu.VMEM((EDGES, L), BF)] * 7
+    edge_rows = [pltpu.VMEM((EDGES, L), BF)] * 9
     pair = lambda *sizes: [pltpu.VMEM(sizes, BF)] * 2
     dma = pltpu.SemaphoreType.DMA
     ins = (
@@ -378,7 +417,8 @@
         scratch_shapes=[pltpu.VMEM(v.shape, v.dtype) for v in ins]
         + edge_rows
         + [
-            pltpu.VMEM((11 * L, 2 * L), BF), pltpu.VMEM((NODES, 2 * L), F32), pltpu.VMEM((10 * L, L), F32),
+            pltpu.VMEM((11 * L, 2 * L), BF), pltpu.VMEM((NODES, 2 * L), F32), pltpu.VMEM((S_HALF, 2 * L), F32),
+            pltpu.VMEM((R_HALF, 2 * L), F32),
             pltpu.VMEM((DEVICES * CAP, NODES), BF),
         ]
         + pair(4, MIRROR, L) + pair(DEVICES, 2 * CAP, L) + pair(DEVICES, CAP, L) * 3 + pair(4, MIRROR, L)

time: 67.2 us -> 62.2 us (0.926)
  Pallas kernels: 66.3 us -> 61.5 us
    pallas_call x1, Pallas kernels: 62.2 us -> 57.4 us  [local(): pl.pallas_call(kernel, out_shape=[shaped(NODES, L), shaped(EDGES, L), sha...]
where the time goes in v2:
time: 62.2 us; the launch traced here: 62.1 us
  Pallas kernels  61.5 us (99%)
  between operations  0.65 us (1%)
    pallas_call x1, Pallas kernels, local(): pl.pallas_call(kernel, out_shape=[shaped(NODES, L), shaped(EDGES, L), sha...  57.4 us
    pallas_call x1, Pallas kernels, local(): pl.pallas_call(finish_kernel, out_shape=[shaped(NODES, L), shaped(EDGES,...  4.09 us

profile of v2, /device:TPU:1, one launch (start us, length us, event | category | flops | bytes accessed | tf_op | source)
XLA Modules:
  0.0 62.1 jit_solution(2843366097450871671)
XLA Ops:
  0.6 57.4 %mesh_layer.1 = (bf16[512,128]{1,0:T(8,128)(2,1)}, bf16[8192,128]{1,0:T(8,128)(2,1)}, bf16[128,128]{1,0:T(8,128)(2,1)}, f32[512,128]{1,0:T(8,128)}, bf16[8192,128]{1,0:T(8,128)(2,1)}, /*index=5*/f32[128,128]{1,0:T(8,128)}) custom-call(s32[1,8192]{1,0:T(1,128)} %bitcast.27, s32[1,8192]{1,0:T(1,128)} %bitcast.28, s32[4,64]{1,0:T(4,128)} %bitcast.31, ...), custom_call_target="tpu_custom_call" | custom-call | tf_op jit(solution)/shard_map/mesh_layer/pallas_call | solution.py:409
  58.0 4.1 %write_results.1 = (bf16[512,128]{1,0:T(8,128)(2,1)}, bf16[8192,128]{1,0:T(8,128)(2,1)}, bf16[128,128]{1,0:T(8,128)(2,1)}, f32[512,128]{1,0:T(8,128)}, f32[8192,128]{1,0:T(8,128)}, /*index=5*/f32[128,128]{1,0:T(8,128)}) custom-call(bf16[512,128]{1,0:T(8,128)(2,1)} %get-tuple-element.18.refs_0_, bf16[8192,128]{1,0:T(8,128)(2,1)} %get-tuple-element.19.refs_1_, ...), custom_call_target="tpu_custom_call" | custom-call | tf_op jit(solution)/shard_map/write_results/pallas_call | solution.py:431

commit v3 on v2

--- a/solution.py
+++ b/solution.py
@@ -92,14 +92,23 @@
     return pl.ds(i * CHUNK if isinstance(i, int) else pl.multiple_of(i * CHUNK, CHUNK), CHUNK)
 
 
-def edge_forward(snd, rcv, lat, table, mixer, gain, norm_o, hid_o, rstd_o, sums, write, between):
+def edge_forward(
+    snd, rcv, lat, s_side, r_side, first, bias, mixer, gain, norm_o, hid_o, rstd_o, code_o, s_upper, r_upper, sums, write, between
+):
     sums[...] = jnp.zeros_like(sums)
 
     def gather(i):
         sl = rows_at(i)
-        s_rows, r_rows = id_code(snd[:, sl]).T, id_code(rcv[:, sl]).T
-        pre = mm(jnp.concatenate([one_hots(s_rows, 6, 1), one_hots(r_rows, 4, 1), lat[sl, :]], 1), table[...])
-        hid_o[sl, :] = jnp.maximum(pre[:, :L] + pre[:, L:], 0.0).astype(BF)
+        for ids, half, upper in ((snd, S_HALF, s_upper), (rcv, R_HALF, r_upper)):
+            flag = jnp.where(ids[:, sl] >= half, 1.0, 0.0).astype(BF)
+            upper[sl, :] = jnp.broadcast_to(flag, (L, CHUNK)).T
+        s_rows, r_rows = id_code(within(snd[:, sl], S_HALF)).T, id_code(within(rcv[:, sl], R_HALF)).T
+        code_o[sl, :] = r_rows
+        src, tgt = mm(one_hots(s_rows, 3, 1), s_side[...]), mm(one_hots(r_rows, 2, 1), r_side[...])
+        src = jnp.where(s_upper[sl, :].astype(F32) > 0, src[:, L:], src[:, :L]).astype(BF)
+        tgt = jnp.where(r_upper[sl, :].astype(F32) > 0, tgt[:, L:], tgt[:, :L]).astype(BF)
+        pre = mm(jnp.concatenate([lat[sl, :], src, tgt], 1), first) + bias
+        hid_o[sl, :] = jnp.maximum(pre, 0.0).astype(BF)
 
     def update(i):
         sl = rows_at(i)
@@ -116,18 +125,6 @@
     staged(gather, update, between)
 
 
-def edge_prepare(snd, rcv, code_o, s_upper, r_upper):
-    def body(i, carry):
-        sl = rows_at(i)
-        for ids, half, upper in ((snd, S_HALF, s_upper), (rcv, R_HALF, r_upper)):
-            flag = jnp.where(ids[:, sl] >= half, 1.0, 0.0).astype(BF)
-            upper[sl, :] = jnp.broadcast_to(flag, (L, CHUNK)).T
-        code_o[sl, :] = id_code(within(rcv[:, sl], R_HALF)).T
-        return carry
-
-    lax.fori_loop(0, STEPS, body, 0)
-
-
 def within(ids, half):
     return jnp.where(ids >= half, ids - half, ids)
 
@@ -183,7 +180,7 @@
     ) = targets
     new_nodes_o, new_edges_o, new_coarse_o, grad_nodes_o, grad_edges_o, grad_coarse_o = refs[INPUTS : INPUTS + 6]
     (
-        norm, hid, rstd, code, new_v, grad_v, cot_pre, s_upper, r_upper, table, sums, s_table, r_table, pick,
+        norm, hid, rstd, code, new_v, grad_v, cot_pre, s_upper, r_upper, s_side, r_side, sums, s_table, r_table, pick,
         mir_out, mir_in, early_out, early_in, mid_out, mid_in, grad_out, grad_in, row_out, row_in, ret_out, ret_in,
         load_sem, new_sem, grad_sem, mir_s, mir_r, ret_s, ret_r, early_s, early_r, mid_s, mid_r,
         gback_s, gback_r, row_s, row_r,
@@ -277,28 +274,27 @@
     exchange(early_out, early_in, early_s, early_r)
 
     w_lat, w_src, w_tgt = e_first[:L, :], e_first[L : 2 * L, :], e_first[2 * L :, :]
-    table[:NODES, :] = halves(mm(fine[...], w_src))
-    table[6 * L : 10 * L, :] = halves(mm(fine[...], w_tgt) + e_bias[...])
-    table[10 * L :, :] = jnp.concatenate([w_lat, jnp.zeros((L, L), BF)], 1)
+    r_side[...] = beside(fine[...])
     second = e_second[...].astype(F32)
     second_mean = jnp.broadcast_to(jnp.mean(second, 1, keepdims=True), (L, L))
     mixer = jnp.concatenate([e_second[...], second_mean.astype(BF)], 1)
     mirror_wait()
-    table[NODES : 6 * L, :] = halves(mm(mir_in[...].reshape(4 * MIRROR, L), w_src))
+    s_side[...] = beside(jnp.concatenate([fine[...], mir_in[...].reshape(4 * MIRROR, L)], 0))
     loads[5].wait()
 
     def write_new(i, sl, value):
         new_v[sl, :] = value
         pltpu.make_async_copy(new_v.at[sl], new_edges_o.at[sl], new_sem.at[i]).start()
 
-    edge_forward(snd, rcv, lat, table, mixer, e_gain[...], norm, hid, rstd, sums, write_new, None)
+    edge_forward(
+        snd, rcv, lat, s_side, r_side, e_first[...], e_bias[...], mixer, e_gain[...], norm, hid, rstd, code, s_upper, r_upper, sums, write_new, None
+    )
 
     summed = sums[:, :L] + sums[:, L:]
     n_hid, n_norm, n_rstd = layer(fine[...], summed, n_first[...], n_bias[...], n_second[...])
     middle = (fine[...].astype(F32) + n_norm * n_gain[...]).astype(BF)
     mid_out[...] = blocks(mm(pick[...], middle)).astype(BF)
     exchange(mid_out, mid_in, mid_s, mid_r)
-    edge_prepare(snd, rcv, code, s_upper, r_upper)
 
     finish(early_out, early_in, early_s, early_r)
     early_rows = early_in[...].astype(F32)
@@ -417,7 +413,7 @@
         scratch_shapes=[pltpu.VMEM(v.shape, v.dtype) for v in ins]
         + edge_rows
         + [
-            pltpu.VMEM((11 * L, 2 * L), BF), pltpu.VMEM((NODES, 2 * L), F32), pltpu.VMEM((S_HALF, 2 * L), F32),
+            pltpu.VMEM((S_HALF, 2 * L), BF), pltpu.VMEM((R_HALF, 2 * L), BF), pltpu.VMEM((NODES, 2 * L), F32), pltpu.VMEM((S_HALF, 2 * L), F32),
             pltpu.VMEM((R_HALF, 2 * L), F32),
             pltpu.VMEM((DEVICES * CAP, NODES), BF),
         ]

time: 62.2 us -> 60.6 us (0.974)
  Pallas kernels: 61.5 us -> 59.8 us
    pallas_call x1, Pallas kernels: 57.4 us -> 55.7 us  [local(): pl.pallas_call(kernel, out_shape=[shaped(NODES, L), shaped(EDGES, L), sha...]
where the time goes in v3:
time: 60.6 us; the launch traced here: 60.5 us
  Pallas kernels  59.8 us (99%)
  between operations  0.65 us (1%)
    pallas_call x1, Pallas kernels, local(): pl.pallas_call(kernel, out_shape=[shaped(NODES, L), shaped(EDGES, L), sha...  55.7 us
    pallas_call x1, Pallas kernels, local(): pl.pallas_call(finish_kernel, out_shape=[shaped(NODES, L), shaped(EDGES,...  4.09 us

profile of v3, /device:TPU:1, one launch (start us, length us, event | category | flops | bytes accessed | tf_op | source)
XLA Modules:
  0.0 60.5 jit_solution(6488678633281969531)
XLA Ops:
  0.6 55.7 %mesh_layer.1 = (bf16[512,128]{1,0:T(8,128)(2,1)}, bf16[8192,128]{1,0:T(8,128)(2,1)}, bf16[128,128]{1,0:T(8,128)(2,1)}, f32[512,128]{1,0:T(8,128)}, bf16[8192,128]{1,0:T(8,128)(2,1)}, /*index=5*/f32[128,128]{1,0:T(8,128)}) custom-call(s32[1,8192]{1,0:T(1,128)} %bitcast.27, s32[1,8192]{1,0:T(1,128)} %bitcast.28, s32[4,64]{1,0:T(4,128)} %bitcast.31, ...), custom_call_target="tpu_custom_call" | custom-call | tf_op jit(solution)/shard_map/mesh_layer/pallas_call | solution.py:405
  56.4 4.1 %write_results.1 = (bf16[512,128]{1,0:T(8,128)(2,1)}, bf16[8192,128]{1,0:T(8,128)(2,1)}, bf16[128,128]{1,0:T(8,128)(2,1)}, f32[512,128]{1,0:T(8,128)}, f32[8192,128]{1,0:T(8,128)}, /*index=5*/f32[128,128]{1,0:T(8,128)}) custom-call(bf16[512,128]{1,0:T(8,128)(2,1)} %get-tuple-element.18.refs_0_, bf16[8192,128]{1,0:T(8,128)(2,1)} %get-tuple-element.19.refs_1_, ...), custom_call_target="tpu_custom_call" | custom-call | tf_op jit(solution)/shard_map/write_results/pallas_call | solution.py:427

commit v4 on v3

--- a/solution.py
+++ b/solution.py
@@ -144,8 +144,8 @@
 
 
 def edge_backward(
-    snd, rcv, code_i, s_upper, r_upper, cot_table, cot, norm_i, hid_i, rstd_i, w_lat, second, gain,
-    s_table, r_table, pre_o, write,
+    snd, rcv, code_i, s_upper, r_upper, cot_table, cot, norm_i, hid_i, rstd_i, second, gain,
+    s_table, r_table, pre_o,
 ):
     s_table[...] = jnp.zeros_like(s_table)
     r_table[...] = jnp.zeros_like(r_table)
@@ -164,7 +164,6 @@
     def spread(i):
         sl = rows_at(i)
         cot_pre = pre_o[sl, :]
-        write(i, sl, (cot[sl, :].astype(F32) + mm_nt(cot_pre, w_lat)).astype(BF))
         s_code, r_code = id_code(within(snd[:, sl], S_HALF)), id_code(within(rcv[:, sl], R_HALF))
         s_table[...] += mm(one_hots(s_code, 3, 0), parted(cot_pre, s_upper[sl, :]))
         r_table[...] += mm(one_hots(r_code, 2, 0), parted(cot_pre, r_upper[sl, :]))
@@ -329,7 +328,7 @@
 
     edge_backward(
         snd, rcv, code, s_upper, r_upper, beside(n_back[:, L:].astype(BF)), cot, norm, hid, rstd,
-        w_lat, second_c, e_gain[...], s_table, r_table, cot_pre, write_grad,
+        second_c, e_gain[...], s_table, r_table, cot_pre,
     )
     back_table = below_each_other(s_table[...]).astype(BF)
     back = mm_nt(back_table[NODES:], w_src)
@@ -337,6 +336,12 @@
     return_wait = mirrors(
         ret_out, ret_in, ret_s, ret_r, ("below", "above", "left", "right"), ("above", "below", "right", "left")
     )
+    def lat_cotangent(i, carry):
+        sl = rows_at(i)
+        write_grad(i, sl, (cot[sl, :].astype(F32) + mm_nt(cot_pre[sl, :], w_lat)).astype(BF))
+        return carry
+
+    lax.fori_loop(0, STEPS, lat_cotangent, 0)
     total = cot_mid + n_back[:, :L] + mm_nt(back_table[:NODES], w_src)
     total = total + mm_nt(below_each_other(r_table[...]).astype(BF), w_tgt)
     finish(row_out, row_in, row_s, row_r)

time: 60.6 us -> 59.8 us (0.987)
  Pallas kernels: 59.8 us -> 59 us
    pallas_call x1, Pallas kernels: 55.7 us -> 54.9 us  [local(): pl.pallas_call(kernel, out_shape=[shaped(NODES, L), shaped(EDGES, L), sha...]
where the time goes in v4:
time: 59.8 us; the launch traced here: 59.7 us
  Pallas kernels  59 us (99%)
  between operations  0.65 us (1%)
    pallas_call x1, Pallas kernels, local(): pl.pallas_call(kernel, out_shape=[shaped(NODES, L), shaped(EDGES, L), sha...  54.9 us
    pallas_call x1, Pallas kernels, local(): pl.pallas_call(finish_kernel, out_shape=[shaped(NODES, L), shaped(EDGES,...  4.09 us

profile of v4, /device:TPU:1, one launch (start us, length us, event | category | flops | bytes accessed | tf_op | source)
XLA Modules:
  0.0 59.7 jit_solution(823644042938020100)
XLA Ops:
  0.6 54.9 %mesh_layer.1 = (bf16[512,128]{1,0:T(8,128)(2,1)}, bf16[8192,128]{1,0:T(8,128)(2,1)}, bf16[128,128]{1,0:T(8,128)(2,1)}, f32[512,128]{1,0:T(8,128)}, bf16[8192,128]{1,0:T(8,128)(2,1)}, /*index=5*/f32[128,128]{1,0:T(8,128)}) custom-call(s32[1,8192]{1,0:T(1,128)} %bitcast.27, s32[1,8192]{1,0:T(1,128)} %bitcast.28, s32[4,64]{1,0:T(4,128)} %bitcast.31, ...), custom_call_target="tpu_custom_call" | custom-call | tf_op jit(solution)/shard_map/mesh_layer/pallas_call | solution.py:410
  55.6 4.1 %write_results.1 = (bf16[512,128]{1,0:T(8,128)(2,1)}, bf16[8192,128]{1,0:T(8,128)(2,1)}, bf16[128,128]{1,0:T(8,128)(2,1)}, f32[512,128]{1,0:T(8,128)}, f32[8192,128]{1,0:T(8,128)}, /*index=5*/f32[128,128]{1,0:T(8,128)}) custom-call(bf16[512,128]{1,0:T(8,128)(2,1)} %get-tuple-element.18.refs_0_, bf16[8192,128]{1,0:T(8,128)(2,1)} %get-tuple-element.19.refs_1_, ...), custom_call_target="tpu_custom_call" | custom-call | tf_op jit(solution)/shard_map/write_results/pallas_call | solution.py:432
